TPU v7x, 256 devices: a whole 4x4x8 slice. The times are simulated.
256 devices in a mesh: freq: 64 (over y, z, x_hi), tm: 4 (over x_lo, core).
Axes of the slice: x: 4 (x_hi: 2, x_lo: 2; x = x_hi * 2 + x_lo), y: 4, z: 8, core: 2. Of those that a mesh axis runs over, the one named last changes fastest.
Arguments:
- voltages: int32 [1024, 32, 2, 4096], P('freq', 'tm'), may hold values from -127 to 127
- tile_map: int32 [36], replicated, may hold values from 0 to 35, each once
Outputs:
- visibilities: float32 [36, 128, 2, 128, 128], P('tm', 'freq')
Inputs may be any that keep to these rules, and one draw needn't show every extreme that they name: `tile_map`: a permutation of the tile ids.
All inputs are finite; a program needn't handle non-finite values.
Results may differ from a plain program's by a relative error of at most 0.0052.
Values may be sent and summed in bfloat16 or wider, within the bound.
A program may use at most 128 MiB of HBM per device.

v0:
```python
import functools
import math

import jax
import jax.numpy as jnp
import numpy as np
from jax import lax
from jax.experimental import pallas as pl
from jax.experimental.pallas import tpu as pltpu
from jax.sharding import PartitionSpec as P

NCHAN = 4096
TAPS = 4
TB = 128
CHANNELS = 128
FIRST = NCHAN // 2 - CHANNELS // 2
CH_DEV = 2
LANES = 128
CHUNKS = NCHAN // LANES
ROWS = 2 * CHUNKS
HALF = ROWS // 2
BLOCKS = 8
OUT = BLOCKS + TAPS - 1
PATHS = 16
SLOT = 16
SPECTRA = 32
QUADS = CHANNELS // 4
MESH = pl.DeviceIdType.MESH


def window_table():
    n = np.arange(TAPS * NCHAN, dtype=np.float64) + 0.5
    taper = 0.5 - 0.5 * np.cos(2.0 * math.pi * n / (TAPS * NCHAN))
    taps = np.sinc(n / NCHAN - TAPS / 2.0) * taper / (128.0 * math.sqrt(NCHAN))
    taps = np.repeat(taps.reshape(TAPS, CHUNKS, 1, LANES), 2, axis=2)
    return taps.reshape(TAPS, ROWS, LANES).astype(np.float32)


def turn_table():
    sample = np.arange(LANES)[:, None]
    m = np.arange(CHANNELS)[None, :]
    angle = (sample * (FIRST + m) % NCHAN) * (2.0 * math.pi / NCHAN)
    first = np.concatenate([np.cos(angle), -np.sin(angle)], axis=1)
    sign = np.tile(1.0 - 2.0 * (m % 2), (1, 2))
    table = np.concatenate([first, first * sign], axis=0).astype(np.float32)
    high = table.astype(jnp.bfloat16)
    low = (table - high.astype(np.float32)).astype(jnp.bfloat16)
    return np.concatenate([high, low], axis=0)


def run_table():
    run = np.arange(HALF)[:, None] // 2
    part = np.arange(HALF)[:, None] % 2
    m = np.arange(CHANNELS)[None, :]
    angle = (run * LANES * (FIRST + m) % NCHAN) * (2.0 * math.pi / NCHAN)
    turned = np.exp(-1j * angle) * np.where(part == 0, 1.0, 1j)
    return np.stack([turned.real, turned.imag]).astype(np.float32)


def quad_table():
    table = np.arange(QUADS)[:, None] == np.arange(CHANNELS)[None, :] // 4
    return table.astype(jnp.bfloat16)


def place_table(times):
    table = np.zeros((times, 2, 2, 2, SLOT, 2, 2, 2, SPECTRA), np.float32)
    for t in range(times):
        for step in range(OUT):
            if t * BLOCKS + step < times * BLOCKS:
                for e in range(2):
                    for c in range(2):
                        for q in range(2):
                            table[t, e, c, q, step, e, c, q, t * BLOCKS + step] = 1.0
    return table.reshape(times * LANES, 2 * LANES).astype(jnp.bfloat16)


def front(
    freqs,
    times,
    x_hbm,
    window,
    turn,
    runs,
    quads,
    place,
    spectra,
    x,
    z,
    sums,
    mixed,
    packed,
    landed,
    ready,
    x_sem,
    slice_send,
    slice_recv,
    own_sem,
    spread_send,
    spread_recv,
):
    f, t = lax.axis_index("freq"), lax.axis_index("tm")
    group = freqs // times
    rows = group // 2 * PATHS
    among = (f // group == t).astype(jnp.int32)
    per_path = BLOCKS * ROWS

    def fetch(i):
        at = pl.ds(pl.multiple_of(i * per_path, per_path), per_path)
        return pltpu.make_async_copy(x_hbm.at[at], x.at[at], x_sem.at[i])

    def start_fetch(i, carry):
        fetch(i).start()
        return carry

    lax.fori_loop(0, PATHS, start_fetch, 0)

    barrier = pltpu.get_barrier_semaphore()
    for d in range(1, times):
        pl.semaphore_signal(
            barrier, inc=1, device_id=(f, lax.rem(t + d, times)), device_id_type=MESH
        )

    def greet(j, carry):
        @pl.when((j != f) | (among == 0))
        def _():
            pl.semaphore_signal(
                barrier, inc=1, device_id=(j, f // group), device_id_type=MESH
            )

        return carry

    lax.fori_loop(0, freqs, greet, 0)
    sums[...] = jnp.zeros_like(sums)

    def channelize(i, carry):
        fetch(i).wait()
        for g in range(ROWS // 16):
            taps = [window[k, g * 16 : (g + 1) * 16, :] for k in range(TAPS)]
            steps = []
            for b in range(BLOCKS):
                at = pl.multiple_of(i * per_path + b * ROWS + g * 16, 16)
                steps.append(x[pl.ds(at, 16), :].astype(jnp.float32))
            for s in range(OUT):
                terms = [
                    taps[k] * steps[s - TAPS + 1 + k]
                    for k in range(TAPS)
                    if 0 <= s - TAPS + 1 + k < BLOCKS
                ]
                total = functools.reduce(lambda a, b: a + b, terms)
                at, side = s * HALF + g % 2 * 16, g // 2 * LANES
                z[at : at + 16, side : side + LANES] = total.astype(jnp.bfloat16)
        value = z[...]
        u = jnp.dot(
            jnp.concatenate([value, value], axis=1),
            turn[...],
            preferred_element_type=jnp.float32,
        )
        real, imag = runs[0], runs[1]
        at = pl.multiple_of(i * 2 * SLOT, 2 * SLOT)
        for s in range(OUT):
            u0 = u[s * HALF : (s + 1) * HALF, :LANES]
            u1 = u[s * HALF : (s + 1) * HALF, LANES:]
            a = jnp.sum(real * u0 - imag * u1, axis=0, keepdims=True)
            b = jnp.sum(imag * u0 + real * u1, axis=0, keepdims=True)
            sums[pl.ds(at + s, 1), :] = a
            sums[pl.ds(at + SLOT + s, 1), :] = b
        return carry

    lax.fori_loop(0, PATHS, channelize, 0)

    of_quad = lax.broadcasted_iota(jnp.int32, (2 * SLOT, LANES), 1) % 4
    for i in range(PATHS):
        value = sums[i * 2 * SLOT : (i + 1) * 2 * SLOT, :]
        four = jnp.concatenate(
            [jnp.where(of_quad == m, value, 0.0) for m in range(4)], axis=0
        ).astype(jnp.bfloat16)
        moved = lax.dot_general(
            quads[...],
            four,
            (((1,), (1,)), ((), ())),
            preferred_element_type=jnp.float32,
        )
        mixed[pl.ds(i, QUADS, stride=PATHS), :] = moved
    packed[...] = mixed[...].astype(jnp.bfloat16)

    pl.semaphore_wait(barrier, times - 1 + freqs - among)
    slices = []
    for d in range(1, times):
        to = lax.rem(t + d, times)
        copy = pltpu.make_async_remote_copy(
            src_ref=packed.at[pl.ds(pl.multiple_of(to * rows, rows), rows)],
            dst_ref=landed.at[t],
            send_sem=slice_send.at[d - 1],
            recv_sem=slice_recv.at[d - 1],
            device_id=(f, to),
            device_id_type=MESH,
        )
        copy.start()
        slices.append(copy)
    landed[t] = packed[pl.ds(pl.multiple_of(t * rows, rows), rows), :]
    for copy in slices:
        copy.wait_recv()

    joined = jnp.dot(
        jnp.concatenate([landed[j] for j in range(times)], axis=1),
        place[...],
        preferred_element_type=jnp.float32,
    ).astype(jnp.bfloat16)
    for e in range(2):
        ready[e] = joined[:, e * LANES : (e + 1) * LANES]

    here = spectra.at[pl.ds(pl.multiple_of(f * PATHS, PATHS), PATHS)]

    def spread(j, carry):
        k = lax.rem(j + f, freqs)
        number, time = k // times, lax.rem(k, times)
        at = pl.ds(pl.multiple_of(number // 2 * PATHS, PATHS), PATHS)
        tile = ready.at[lax.rem(number, 2), at]
        to = t * group + number
        local = (to == f) & (time == t)

        @pl.when(local)
        def _():
            pltpu.make_async_copy(tile, here, own_sem).start()

        @pl.when(jnp.logical_not(local))
        def _():
            pltpu.make_async_remote_copy(
                src_ref=tile,
                dst_ref=here,
                send_sem=spread_send,
                recv_sem=spread_recv,
                device_id=(to, time),
                device_id_type=MESH,
            ).start()

        return carry

    lax.fori_loop(0, freqs, spread, 0)
    for copy in slices:
        copy.wait_send()

    def drain(count):
        some = spectra.at[pl.ds(0, count * PATHS)]
        pltpu.make_async_copy(some, some, spread_send).wait()
        pltpu.make_async_copy(some, some, spread_recv).wait()

    @pl.when(among == 1)
    def _():
        tile = ready.at[0, pl.ds(0, PATHS)]
        pltpu.make_async_copy(tile, here, own_sem).wait()
        drain(freqs - 1)

    @pl.when(among == 0)
    def _():
        drain(freqs)


def correlate(slots, ids, spectra, out, tiles, sems):
    t = lax.axis_index("tm")
    lane = lax.broadcasted_iota(jnp.int32, (TB, LANES), 1)
    first = lane < LANES // 2
    even = lane // SPECTRA % 2 == 0
    for j in range(slots):
        number = ids[t * slots + j]
        row = jnp.int32(0)
        for k in range(1, 8):
            row = row + (number >= k * (k + 1) // 2).astype(jnp.int32)
        col = number - row * (row + 1) // 2
        left = spectra[pl.ds(pl.multiple_of(row * TB, TB), TB), :].astype(jnp.float32)
        right = spectra[pl.ds(pl.multiple_of(col * TB, TB), TB), :]
        turned = jnp.where(
            even,
            pltpu.roll(left, LANES - SPECTRA, 1),
            -pltpu.roll(left, SPECTRA, 1),
        )
        four = jnp.concatenate(
            [
                jnp.where(first, left, 0.0),
                jnp.where(first, turned, 0.0),
                jnp.where(first, 0.0, left),
                jnp.where(first, 0.0, turned),
            ],
            axis=0,
        ).astype(jnp.bfloat16)
        products = lax.dot_general(
            four, right, (((1,), (1,)), ((), ())), preferred_element_type=jnp.float32
        )
        tiles[j] = (products * (1.0 / SPECTRA)).reshape(CH_DEV, 2, TB, TB)
        pltpu.make_async_copy(tiles.at[j], out.at[j], sems.at[j]).start()
    for j in range(slots):
        pltpu.make_async_copy(tiles.at[j], out.at[j], sems.at[j]).wait()


def run_front(freqs, times, samples):
    rows = freqs // times // 2 * PATHS
    dma = pltpu.SemaphoreType.DMA
    vmem = pl.BlockSpec(memory_space=pltpu.VMEM)
    return pl.pallas_call(
        functools.partial(front, freqs, times),
        out_shape=jax.ShapeDtypeStruct((freqs * PATHS, LANES), jnp.bfloat16),
        in_specs=[pl.BlockSpec(memory_space=pltpu.HBM)] + [vmem] * 5,
        out_specs=pl.BlockSpec(memory_space=pl.ANY),
        scratch_shapes=[
            pltpu.VMEM((PATHS * BLOCKS * ROWS, LANES), jnp.int32),
            pltpu.VMEM((OUT * HALF, 2 * LANES), jnp.bfloat16),
            pltpu.VMEM((PATHS * 2 * SLOT, LANES), jnp.float32),
            pltpu.VMEM((QUADS * PATHS, LANES), jnp.float32),
            pltpu.VMEM((QUADS * PATHS, LANES), jnp.bfloat16),
            pltpu.VMEM((times, rows, LANES), jnp.bfloat16),
            pltpu.VMEM((2, rows, LANES), jnp.bfloat16),
            dma((PATHS,)),
            dma((times - 1,)),
            dma((times - 1,)),
            dma,
            dma,
            dma,
        ],
        compiler_params=pltpu.CompilerParams(
            collective_id=0, has_side_effects=True, vmem_limit_bytes=60 * 2**20
        ),
        name="front",
    )(
        samples,
        jnp.asarray(window_table()),
        jnp.asarray(turn_table()),
        jnp.asarray(run_table()),
        jnp.asarray(quad_table()),
        jnp.asarray(place_table(times)),
    )


def run_correlate(slots, tile_map, spectra):
    return pl.pallas_call(
        functools.partial(correlate, slots),
        out_shape=jax.ShapeDtypeStruct((slots, CH_DEV, 2, TB, TB), jnp.float32),
        in_specs=[
            pl.BlockSpec(memory_space=pltpu.SMEM),
            pl.BlockSpec(memory_space=pltpu.VMEM),
        ],
        out_specs=pl.BlockSpec(memory_space=pl.ANY),
        scratch_shapes=[
            pltpu.VMEM((slots, CH_DEV, 2, TB, TB), jnp.float32),
            pltpu.SemaphoreType.DMA((slots,)),
        ],
        compiler_params=pltpu.CompilerParams(vmem_limit_bytes=40 * 2**20),
        name="correlate",
    )(tile_map, spectra)


def on_device(voltages, tile_map):
    freqs, times = lax.axis_size("freq"), lax.axis_size("tm")
    samples = voltages.reshape(PATHS, BLOCKS, 2, CHUNKS, LANES)
    samples = samples.transpose(0, 1, 3, 2, 4).reshape(PATHS * BLOCKS * ROWS, LANES)
    spectra = run_front(freqs, times, samples)
    return run_correlate(tile_map.shape[0] // times, tile_map, spectra)


def solution(mesh):
    in_specs = (P("freq", "tm", None, None), P())
    out_specs = P("tm", "freq", None, None, None)
    return jax.shard_map(
        on_device, mesh=mesh, in_specs=in_specs, out_specs=out_specs, check_vma=False
    )
```

profile of v0, /device:TPU:1, one launch (start us, length us, event | category | flops | bytes accessed | tf_op | source)
XLA Modules:
  0.0 33.6 jit_solution(4366051746563107977)
XLA Ops:
  0.0 0.0 copy-start.1
  0.0 30.4 %front.1.spectra = bf16[1024,128]{1,0:T(8,128)(2,1)} custom-call(s32[8192,128]{1,0:T(8,128)} %bitcast.5, f32[4,64,128]{2,1,0:T(8,128)} %constant.10.clone.window, bf16[512,256]{1,0:T(8,128)(2,1)} %constant.11.clone.turn, f32[2,32,128]{2,1,0:T(8,128)} %constant.12.clone.runs, bf16[32,128]{1,0:T(8,128)(2,1)} %constant.13.clone.quads, ...), custom_call_target="tpu_custom_call" | custom-call | tf_op jit(solution)/shard_map/front/pallas_call | solution.py:299
  30.4 0.0 copy-done.1
  30.4 0.0 copy-start
  30.4 0.9 %copy-done = bf16[1024,128]{1,0:T(8,128)(2,1)S(1)} copy-done((bf16[1024,128]{1,0:T(8,128)(2,1)S(1)}, bf16[1024,128]{1,0:T(8,128)(2,1)}, u32[]{:S(2)}) %copy-start) | copy-done | bytes 262168
  31.4 2.3 %correlate.1 = f32[9,2,2,128,128]{4,3,2,1,0:T(8,128)} custom-call(s32[36]{0:T(128)S(1)} %copy-done.1, bf16[1024,128]{1,0:T(8,128)(2,1)S(1)} %copy-done), custom_call_target="tpu_custom_call" | custom-call | tf_op jit(solution)/shard_map/correlate/pallas_call | solution.py:334
Async XLA Ops:
  0.0 30.4 %copy-start.1 = (s32[36]{0:T(128)S(1)}, s32[36]{0:T(128)}, u32[]{:S(2)}) copy-start(s32[36]{0:T(128)} %ids.1) | copy-start | bytes 436
  30.4 1.0 %copy-start = (bf16[1024,128]{1,0:T(8,128)(2,1)S(1)}, bf16[1024,128]{1,0:T(8,128)(2,1)}, u32[]{:S(2)}) copy-start(bf16[1024,128]{1,0:T(8,128)(2,1)} %front.1.spectra) | copy-start | bytes 786436
where the time goes:
time: 33.8 us; the launch traced here: 33.6 us
  Pallas kernels  32.7 us (97%)
  local copies, waits for them, and re-layouts  0.95 us (3%)
    pallas_call x1, Pallas kernels, run_front(): pl.pallas_call(functools.partial(front, freqs, times), out_shape=jax.Shap...  30.4 us
    pallas_call x1, Pallas kernels, run_correlate(): pl.pallas_call(functools.partial(correlate, slots), out_shape=jax.ShapeDt...  2.26 us
    unnamed x4, local copies, waits for them, and re-layouts  0.95 us

commit v1 on v0

--- a/solution.py
+++ b/solution.py
@@ -25,6 +25,8 @@
 SLOT = 16
 SPECTRA = 32
 QUADS = CHANNELS // 4
+BATCH = 4
+PARTS = 4
 MESH = pl.DeviceIdType.MESH
 
 
@@ -78,13 +80,18 @@
     freqs,
     times,
     x_hbm,
+    window_hbm,
+    turn_hbm,
+    runs_hbm,
+    quads_hbm,
+    place_hbm,
+    spectra,
+    x,
     window,
     turn,
     runs,
     quads,
     place,
-    spectra,
-    x,
     z,
     sums,
     mixed,
@@ -92,16 +99,20 @@
     landed,
     ready,
     x_sem,
+    table_sem,
     slice_send,
     slice_recv,
-    own_sem,
     spread_send,
     spread_recv,
+    share_send,
+    share_recv,
 ):
     f, t = lax.axis_index("freq"), lax.axis_index("tm")
     group = freqs // times
     rows = group // 2 * PATHS
-    among = (f // group == t).astype(jnp.int32)
+    half = freqs // 2
+    core, mine = f // half, lax.rem(t, 2)
+    among = ((f // group == t) & (core == mine)).astype(jnp.int32)
     per_path = BLOCKS * ROWS
 
     def fetch(i):
@@ -112,7 +123,20 @@
         fetch(i).start()
         return carry
 
-    lax.fori_loop(0, PATHS, start_fetch, 0)
+    tables = [
+        pltpu.make_async_copy(source, target, table_sem.at[k])
+        for k, (source, target) in enumerate(
+            zip(
+                (window_hbm, turn_hbm, runs_hbm, quads_hbm, place_hbm),
+                (window, turn, runs, quads, place),
+            )
+        )
+    ]
+    tables[0].start()
+    lax.fori_loop(0, BATCH, start_fetch, 0)
+    for table in tables[1:]:
+        table.start()
+    lax.fori_loop(BATCH, PATHS, start_fetch, 0)
 
     barrier = pltpu.get_barrier_semaphore()
     for d in range(1, times):
@@ -121,34 +145,62 @@
         )
 
     def greet(j, carry):
-        @pl.when((j != f) | (among == 0))
+        source = half * mine + j
+
+        @pl.when((source != f) | (f // group != t))
         def _():
             pl.semaphore_signal(
-                barrier, inc=1, device_id=(j, f // group), device_id_type=MESH
+                barrier, inc=1, device_id=(source, f // group), device_id_type=MESH
             )
 
         return carry
 
-    lax.fori_loop(0, freqs, greet, 0)
+    lax.fori_loop(0, half, greet, 0)
     sums[...] = jnp.zeros_like(sums)
 
-    def channelize(i, carry):
-        fetch(i).wait()
-        for g in range(ROWS // 16):
-            taps = [window[k, g * 16 : (g + 1) * 16, :] for k in range(TAPS)]
-            steps = []
-            for b in range(BLOCKS):
-                at = pl.multiple_of(i * per_path + b * ROWS + g * 16, 16)
-                steps.append(x[pl.ds(at, 16), :].astype(jnp.float32))
-            for s in range(OUT):
-                terms = [
-                    taps[k] * steps[s - TAPS + 1 + k]
+    tables[0].wait()
+
+    def channelize(n, carry):
+        def filtered(j, carry):
+            path, pair = j // 2, lax.rem(j, 2) * 16
+
+            @pl.when(pair == 0)
+            def _():
+                fetch(n * BATCH + path).wait()
+
+            for h in range(2):
+                rows_at = h * HALF + pair
+                start = (n * BATCH + path) * per_path + rows_at
+                taps = [
+                    window[k, pl.ds(pl.multiple_of(rows_at, 16), 16), :]
                     for k in range(TAPS)
-                    if 0 <= s - TAPS + 1 + k < BLOCKS
                 ]
-                total = functools.reduce(lambda a, b: a + b, terms)
-                at, side = s * HALF + g % 2 * 16, g // 2 * LANES
-                z[at : at + 16, side : side + LANES] = total.astype(jnp.bfloat16)
+                steps = [
+                    x[pl.ds(pl.multiple_of(start + b * ROWS, 16), 16), :].astype(
+                        jnp.float32
+                    )
+                    for b in range(BLOCKS)
+                ]
+                for s in range(OUT):
+                    terms = [
+                        taps[k] * steps[s - TAPS + 1 + k]
+                        for k in range(TAPS)
+                        if 0 <= s - TAPS + 1 + k < BLOCKS
+                    ]
+                    total = functools.reduce(lambda a, b: a + b, terms)
+                    at = pl.multiple_of((path * OUT + s) * HALF + pair, 16)
+                    z[pl.ds(at, 16), h * LANES : (h + 1) * LANES] = total.astype(
+                        jnp.bfloat16
+                    )
+            return carry
+
+        lax.fori_loop(0, 2 * BATCH, filtered, 0)
+
+        @pl.when(n == 0)
+        def _():
+            tables[1].wait()
+            tables[2].wait()
+
         value = z[...]
         u = jnp.dot(
             jnp.concatenate([value, value], axis=1),
@@ -156,17 +208,20 @@
             preferred_element_type=jnp.float32,
         )
         real, imag = runs[0], runs[1]
-        at = pl.multiple_of(i * 2 * SLOT, 2 * SLOT)
-        for s in range(OUT):
-            u0 = u[s * HALF : (s + 1) * HALF, :LANES]
-            u1 = u[s * HALF : (s + 1) * HALF, LANES:]
-            a = jnp.sum(real * u0 - imag * u1, axis=0, keepdims=True)
-            b = jnp.sum(imag * u0 + real * u1, axis=0, keepdims=True)
-            sums[pl.ds(at + s, 1), :] = a
-            sums[pl.ds(at + SLOT + s, 1), :] = b
+        for path in range(BATCH):
+            at = pl.multiple_of((n * BATCH + path) * 2 * SLOT, 2 * SLOT)
+            for s in range(OUT):
+                k = (path * OUT + s) * HALF
+                u0, u1 = u[k : k + HALF, :LANES], u[k : k + HALF, LANES:]
+                a = jnp.sum(real * u0 - imag * u1, axis=0, keepdims=True)
+                b = jnp.sum(imag * u0 + real * u1, axis=0, keepdims=True)
+                sums[pl.ds(at + s, 1), :] = a
+                sums[pl.ds(at + SLOT + s, 1), :] = b
         return carry
 
-    lax.fori_loop(0, PATHS, channelize, 0)
+    lax.fori_loop(0, PATHS // BATCH, channelize, 0)
+    tables[3].wait()
+    tables[4].wait()
 
     of_quad = lax.broadcasted_iota(jnp.int32, (2 * SLOT, LANES), 1) % 4
     for i in range(PATHS):
@@ -183,7 +238,7 @@
         mixed[pl.ds(i, QUADS, stride=PATHS), :] = moved
     packed[...] = mixed[...].astype(jnp.bfloat16)
 
-    pl.semaphore_wait(barrier, times - 1 + freqs - among)
+    pl.semaphore_wait(barrier, times - 1 + 2 * group - among)
     slices = []
     for d in range(1, times):
         to = lax.rem(t + d, times)
@@ -210,10 +265,12 @@
         ready[e] = joined[:, e * LANES : (e + 1) * LANES]
 
     here = spectra.at[pl.ds(pl.multiple_of(f * PATHS, PATHS), PATHS)]
+    part = half // PARTS
+    arrived = spread_recv.at[lax.rem(f // part, PARTS)]
 
     def spread(j, carry):
-        k = lax.rem(j + f, freqs)
-        number, time = k // times, lax.rem(k, times)
+        k = lax.rem(j + f, 2 * group)
+        number, time = k // 2, 2 * lax.rem(k, 2) + core
         at = pl.ds(pl.multiple_of(number // 2 * PATHS, PATHS), PATHS)
         tile = ready.at[lax.rem(number, 2), at]
         to = t * group + number
@@ -221,7 +278,7 @@
 
         @pl.when(local)
         def _():
-            pltpu.make_async_copy(tile, here, own_sem).start()
+            pltpu.make_async_copy(tile, here, arrived).start()
 
         @pl.when(jnp.logical_not(local))
         def _():
@@ -229,31 +286,48 @@
                 src_ref=tile,
                 dst_ref=here,
                 send_sem=spread_send,
-                recv_sem=spread_recv,
+                recv_sem=arrived,
                 device_id=(to, time),
                 device_id_type=MESH,
             ).start()
 
         return carry
 
-    lax.fori_loop(0, freqs, spread, 0)
+    lax.fori_loop(0, 2 * group, spread, 0)
+
+    mate = t + 1 - 2 * mine
+    shared = []
+    for k in range(PARTS):
+        at = (mine * PARTS + k) * part * PATHS
+        some = spectra.at[pl.ds(pl.multiple_of(at, part * PATHS), part * PATHS)]
+        pltpu.make_async_copy(some, some, spread_recv.at[k]).wait()
+        copy = pltpu.make_async_remote_copy(
+            src_ref=some,
+            dst_ref=some,
+            send_sem=share_send.at[k],
+            recv_sem=share_recv.at[k],
+            device_id=(f, mate),
+            device_id_type=MESH,
+        )
+        copy.start()
+        shared.append(copy)
     for copy in slices:
         copy.wait_send()
 
     def drain(count):
         some = spectra.at[pl.ds(0, count * PATHS)]
         pltpu.make_async_copy(some, some, spread_send).wait()
-        pltpu.make_async_copy(some, some, spread_recv).wait()
 
     @pl.when(among == 1)
     def _():
-        tile = ready.at[0, pl.ds(0, PATHS)]
-        pltpu.make_async_copy(tile, here, own_sem).wait()
-        drain(freqs - 1)
+        drain(2 * group - 1)
 
     @pl.when(among == 0)
     def _():
-        drain(freqs)
+        drain(2 * group)
+
+    for copy in shared:
+        copy.wait()
 
 
 def correlate(slots, ids, spectra, out, tiles, sems):
@@ -295,39 +369,42 @@
 def run_front(freqs, times, samples):
     rows = freqs // times // 2 * PATHS
     dma = pltpu.SemaphoreType.DMA
-    vmem = pl.BlockSpec(memory_space=pltpu.VMEM)
+    hbm = pl.BlockSpec(memory_space=pl.ANY)
+    tables = [
+        window_table(),
+        turn_table(),
+        run_table(),
+        quad_table(),
+        place_table(times),
+    ]
     return pl.pallas_call(
         functools.partial(front, freqs, times),
         out_shape=jax.ShapeDtypeStruct((freqs * PATHS, LANES), jnp.bfloat16),
-        in_specs=[pl.BlockSpec(memory_space=pltpu.HBM)] + [vmem] * 5,
-        out_specs=pl.BlockSpec(memory_space=pl.ANY),
+        in_specs=[hbm] * (1 + len(tables)),
+        out_specs=hbm,
         scratch_shapes=[
             pltpu.VMEM((PATHS * BLOCKS * ROWS, LANES), jnp.int32),
-            pltpu.VMEM((OUT * HALF, 2 * LANES), jnp.bfloat16),
+            *[pltpu.VMEM(table.shape, table.dtype) for table in tables],
+            pltpu.VMEM((BATCH * OUT * HALF, 2 * LANES), jnp.bfloat16),
             pltpu.VMEM((PATHS * 2 * SLOT, LANES), jnp.float32),
             pltpu.VMEM((QUADS * PATHS, LANES), jnp.float32),
             pltpu.VMEM((QUADS * PATHS, LANES), jnp.bfloat16),
             pltpu.VMEM((times, rows, LANES), jnp.bfloat16),
             pltpu.VMEM((2, rows, LANES), jnp.bfloat16),
             dma((PATHS,)),
+            dma((len(tables),)),
             dma((times - 1,)),
             dma((times - 1,)),
             dma,
-            dma,
-            dma,
+            dma((PARTS,)),
+            dma((PARTS,)),
+            dma((PARTS,)),
         ],
         compiler_params=pltpu.CompilerParams(
             collective_id=0, has_side_effects=True, vmem_limit_bytes=60 * 2**20
         ),
         name="front",
-    )(
-        samples,
-        jnp.asarray(window_table()),
-        jnp.asarray(turn_table()),
-        jnp.asarray(run_table()),
-        jnp.asarray(quad_table()),
-        jnp.asarray(place_table(times)),
-    )
+    )(samples, *[jnp.asarray(table) for table in tables])
 
 
 def run_correlate(slots, tile_map, spectra):

time: 33.8 us -> 30.7 us (0.908)
  Pallas kernels: 32.7 us -> 29.6 us
    pallas_call x1, Pallas kernels: 30.4 us -> 27.3 us  [run_front(): pl.pallas_call(functools.partial(front, freqs, times), out_shape=jax.Shap...]
where the time goes in v1:
time: 30.7 us; the launch traced here: 30.6 us
  Pallas kernels  29.6 us (96%)
  local copies, waits for them, and re-layouts  0.95 us (3%)
    pallas_call x1, Pallas kernels, run_front(): pl.pallas_call(functools.partial(front, freqs, times), out_shape=jax.Shap...  27.3 us
    pallas_call x1, Pallas kernels, run_correlate(): pl.pallas_call(functools.partial(correlate, slots), out_shape=jax.ShapeDt...  2.26 us
    unnamed x4, local copies, waits for them, and re-layouts  0.95 us

profile of v1, /device:TPU:1, one launch (start us, length us, event | category | flops | bytes accessed | tf_op | source)
XLA Modules:
  0.0 30.6 jit_solution(2101035924261038878)
XLA Ops:
  0.0 0.0 copy-start.1
  0.0 27.3 %front.1.spectra = bf16[1024,128]{1,0:T(8,128)(2,1)} custom-call(s32[8192,128]{1,0:T(8,128)} %bitcast.5, f32[4,64,128]{2,1,0:T(8,128)} %constant.10.clone.window_hbm, bf16[512,256]{1,0:T(8,128)(2,1)} %constant.11.clone.turn_hbm, f32[2,32,128]{2,1,0:T(8,128)} %constant.12.clone.runs_hbm, bf16[32,128]{1,0:T(8,128)(2,1)} %constant.13.clone.quads_hbm, ...), custom_call_target="tpu_custom_call" | custom-call | tf_op jit(solution)/shard_map/front/pallas_call | solution.py:380
  27.4 0.0 copy-done.1
  27.4 0.0 copy-start
  27.4 0.9 %copy-done = bf16[1024,128]{1,0:T(8,128)(2,1)S(1)} copy-done((bf16[1024,128]{1,0:T(8,128)(2,1)S(1)}, bf16[1024,128]{1,0:T(8,128)(2,1)}, u32[]{:S(2)}) %copy-start) | copy-done | bytes 262168
  28.3 2.3 %correlate.1 = f32[9,2,2,128,128]{4,3,2,1,0:T(8,128)} custom-call(s32[36]{0:T(128)S(1)} %copy-done.1, bf16[1024,128]{1,0:T(8,128)(2,1)S(1)} %copy-done), custom_call_target="tpu_custom_call" | custom-call | tf_op jit(solution)/shard_map/correlate/pallas_call | solution.py:411
Async XLA Ops:
  0.0 27.4 %copy-start.1 = (s32[36]{0:T(128)S(1)}, s32[36]{0:T(128)}, u32[]{:S(2)}) copy-start(s32[36]{0:T(128)} %ids.1) | copy-start | bytes 436
  27.4 1.0 %copy-start = (bf16[1024,128]{1,0:T(8,128)(2,1)S(1)}, bf16[1024,128]{1,0:T(8,128)(2,1)}, u32[]{:S(2)}) copy-start(bf16[1024,128]{1,0:T(8,128)(2,1)} %front.1.spectra) | copy-start | bytes 786436

commit v2 on v1

--- a/solution.py
+++ b/solution.py
@@ -18,14 +18,15 @@
 LANES = 128
 CHUNKS = NCHAN // LANES
 ROWS = 2 * CHUNKS
-HALF = ROWS // 2
+PARTIAL = 16
+FOLD = ROWS // PARTIAL
 BLOCKS = 8
 OUT = BLOCKS + TAPS - 1
 PATHS = 16
 SLOT = 16
 SPECTRA = 32
 QUADS = CHANNELS // 4
-BATCH = 4
+BATCH = 8
 PARTS = 4
 MESH = pl.DeviceIdType.MESH
 
@@ -42,17 +43,25 @@
     sample = np.arange(LANES)[:, None]
     m = np.arange(CHANNELS)[None, :]
     angle = (sample * (FIRST + m) % NCHAN) * (2.0 * math.pi / NCHAN)
-    first = np.concatenate([np.cos(angle), -np.sin(angle)], axis=1)
-    sign = np.tile(1.0 - 2.0 * (m % 2), (1, 2))
-    table = np.concatenate([first, first * sign], axis=0).astype(np.float32)
+    real, imag = np.cos(angle), -np.sin(angle)
+    quarters = []
+    for h in range(FOLD):
+        turns = h * (NCHAN // FOLD) * (FIRST + m) % NCHAN // (NCHAN // FOLD)
+        cosine, sine = (np.array(v)[turns] for v in ((1, 0, -1, 0), (0, -1, 0, 1)))
+        quarters.append(
+            np.concatenate(
+                [real * cosine - imag * sine, real * sine + imag * cosine], axis=1
+            )
+        )
+    table = np.concatenate(quarters, axis=0).astype(np.float32)
     high = table.astype(jnp.bfloat16)
     low = (table - high.astype(np.float32)).astype(jnp.bfloat16)
     return np.concatenate([high, low], axis=0)
 
 
 def run_table():
-    run = np.arange(HALF)[:, None] // 2
-    part = np.arange(HALF)[:, None] % 2
+    run = np.arange(PARTIAL)[:, None] // 2
+    part = np.arange(PARTIAL)[:, None] % 2
     m = np.arange(CHANNELS)[None, :]
     angle = (run * LANES * (FIRST + m) % NCHAN) * (2.0 * math.pi / NCHAN)
     turned = np.exp(-1j * angle) * np.where(part == 0, 1.0, 1j)
@@ -161,24 +170,17 @@
     tables[0].wait()
 
     def channelize(n, carry):
-        def filtered(j, carry):
-            path, pair = j // 2, lax.rem(j, 2) * 16
-
-            @pl.when(pair == 0)
-            def _():
-                fetch(n * BATCH + path).wait()
-
-            for h in range(2):
-                rows_at = h * HALF + pair
-                start = (n * BATCH + path) * per_path + rows_at
+        def filtered(path, carry):
+            fetch(n * BATCH + path).wait()
+            for h in range(FOLD):
+                start = (n * BATCH + path) * per_path + h * PARTIAL
                 taps = [
-                    window[k, pl.ds(pl.multiple_of(rows_at, 16), 16), :]
-                    for k in range(TAPS)
+                    window[k, h * PARTIAL : (h + 1) * PARTIAL, :] for k in range(TAPS)
                 ]
                 steps = [
-                    x[pl.ds(pl.multiple_of(start + b * ROWS, 16), 16), :].astype(
-                        jnp.float32
-                    )
+                    x[
+                        pl.ds(pl.multiple_of(start + b * ROWS, PARTIAL), PARTIAL), :
+                    ].astype(jnp.float32)
                     for b in range(BLOCKS)
                 ]
                 for s in range(OUT):
@@ -188,13 +190,13 @@
                         if 0 <= s - TAPS + 1 + k < BLOCKS
                     ]
                     total = functools.reduce(lambda a, b: a + b, terms)
-                    at = pl.multiple_of((path * OUT + s) * HALF + pair, 16)
-                    z[pl.ds(at, 16), h * LANES : (h + 1) * LANES] = total.astype(
+                    at = pl.multiple_of((path * OUT + s) * PARTIAL, PARTIAL)
+                    z[pl.ds(at, PARTIAL), h * LANES : (h + 1) * LANES] = total.astype(
                         jnp.bfloat16
                     )
             return carry
 
-        lax.fori_loop(0, 2 * BATCH, filtered, 0)
+        lax.fori_loop(0, BATCH, filtered, 0)
 
         @pl.when(n == 0)
         def _():
@@ -211,8 +213,8 @@
         for path in range(BATCH):
             at = pl.multiple_of((n * BATCH + path) * 2 * SLOT, 2 * SLOT)
             for s in range(OUT):
-                k = (path * OUT + s) * HALF
-                u0, u1 = u[k : k + HALF, :LANES], u[k : k + HALF, LANES:]
+                k = (path * OUT + s) * PARTIAL
+                u0, u1 = u[k : k + PARTIAL, :LANES], u[k : k + PARTIAL, LANES:]
                 a = jnp.sum(real * u0 - imag * u1, axis=0, keepdims=True)
                 b = jnp.sum(imag * u0 + real * u1, axis=0, keepdims=True)
                 sums[pl.ds(at + s, 1), :] = a
@@ -379,13 +381,13 @@
     ]
     return pl.pallas_call(
         functools.partial(front, freqs, times),
-        out_shape=jax.ShapeDtypeStruct((freqs * PATHS, LANES), jnp.bfloat16),
+        out_shape=pltpu.VMEM((freqs * PATHS, LANES), jnp.bfloat16),
         in_specs=[hbm] * (1 + len(tables)),
         out_specs=hbm,
         scratch_shapes=[
             pltpu.VMEM((PATHS * BLOCKS * ROWS, LANES), jnp.int32),
             *[pltpu.VMEM(table.shape, table.dtype) for table in tables],
-            pltpu.VMEM((BATCH * OUT * HALF, 2 * LANES), jnp.bfloat16),
+            pltpu.VMEM((BATCH * OUT * PARTIAL, FOLD * LANES), jnp.bfloat16),
             pltpu.VMEM((PATHS * 2 * SLOT, LANES), jnp.float32),
             pltpu.VMEM((QUADS * PATHS, LANES), jnp.float32),
             pltpu.VMEM((QUADS * PATHS, LANES), jnp.bfloat16),

time: 30.7 us -> 28.5 us (0.928)
  Pallas kernels: 29.6 us -> 28.4 us
  local copies, waits for them, and re-layouts: 0.95 us -> 0.01 us
    pallas_call x1, Pallas kernels: 27.3 us -> 26.1 us  [run_front(): pl.pallas_call(functools.partial(front, freqs, times), out_shape=pltpu.VM...]
    unnamed x4 -> x2, local copies, waits for them, and re-layouts: 0.95 us -> 0.01 us
where the time goes in v2:
time: 28.5 us; the launch traced here: 28.4 us
  Pallas kernels  28.4 us (100%)
    pallas_call x1, Pallas kernels, run_front(): pl.pallas_call(functools.partial(front, freqs, times), out_shape=pltpu.VM...  26.1 us
    pallas_call x1, Pallas kernels, run_correlate(): pl.pallas_call(functools.partial(correlate, slots), out_shape=jax.ShapeDt...  2.26 us

profile of v2, /device:TPU:1, one launch (start us, length us, event | category | flops | bytes accessed | tf_op | source)
XLA Modules:
  0.0 28.4 jit_solution(985219342024492541)
XLA Ops:
  0.0 0.0 copy-start
  0.0 26.1 %front.1.spectra = bf16[1024,128]{1,0:T(8,128)(2,1)S(1)} custom-call(s32[8192,128]{1,0:T(8,128)} %bitcast.5, f32[4,64,128]{2,1,0:T(8,128)} %constant.10.clone.window_hbm, bf16[1024,256]{1,0:T(8,128)(2,1)} %constant.11.clone.turn_hbm, f32[2,16,128]{2,1,0:T(8,128)} %constant.12.clone.runs_hbm, bf16[32,128]{1,0:T(8,128)(2,1)} %constant.13.clone.quads_hbm, ...), custom_call_target="tpu_custom_call" | custom-call | tf_op jit(solution)/shard_map/front/pallas_call | solution.py:382
  26.2 0.0 copy-done
  26.2 2.3 %correlate.1 = f32[9,2,2,128,128]{4,3,2,1,0:T(8,128)} custom-call(s32[36]{0:T(128)S(1)} %copy-done, bf16[1024,128]{1,0:T(8,128)(2,1)S(1)} %front.1.spectra), custom_call_target="tpu_custom_call" | custom-call | tf_op jit(solution)/shard_map/correlate/pallas_call | solution.py:413
Async XLA Ops:
  0.0 26.2 %copy-start = (s32[36]{0:T(128)S(1)}, s32[36]{0:T(128)}, u32[]{:S(2)}) copy-start(s32[36]{0:T(128)} %ids.1) | copy-start | bytes 436

commit v3 on v2

--- a/solution.py
+++ b/solution.py
@@ -27,6 +27,7 @@
 SPECTRA = 32
 QUADS = CHANNELS // 4
 BATCH = 8
+PIECES = 2
 PARTS = 4
 MESH = pl.DeviceIdType.MESH
 
@@ -238,64 +239,77 @@
             preferred_element_type=jnp.float32,
         )
         mixed[pl.ds(i, QUADS, stride=PATHS), :] = moved
-    packed[...] = mixed[...].astype(jnp.bfloat16)
+    columns = group // 2
+    z_here = lax.rem(f // 2, columns)
+    far_first = [
+        lax.rem(z_here + d, columns)
+        for d in sorted(range(columns), key=lambda d: -min(d, columns - d))
+    ]
+    for to in range(times):
+        for n, column in enumerate(far_first):
+            at = pl.multiple_of((to * columns + column) * PATHS, PATHS)
+            tile = mixed[pl.ds(at, PATHS), :]
+            at = to * rows + n * PATHS
+            packed[at : at + PATHS, :] = tile.astype(jnp.bfloat16)
 
     pl.semaphore_wait(barrier, times - 1 + 2 * group - among)
-    slices = []
-    for d in range(1, times):
-        to = lax.rem(t + d, times)
-        copy = pltpu.make_async_remote_copy(
-            src_ref=packed.at[pl.ds(pl.multiple_of(to * rows, rows), rows)],
-            dst_ref=landed.at[t],
-            send_sem=slice_send.at[d - 1],
-            recv_sem=slice_recv.at[d - 1],
-            device_id=(f, to),
-            device_id_type=MESH,
-        )
-        copy.start()
-        slices.append(copy)
-    landed[t] = packed[pl.ds(pl.multiple_of(t * rows, rows), rows), :]
-    for copy in slices:
-        copy.wait_recv()
-
-    joined = jnp.dot(
-        jnp.concatenate([landed[j] for j in range(times)], axis=1),
-        place[...],
-        preferred_element_type=jnp.float32,
-    ).astype(jnp.bfloat16)
-    for e in range(2):
-        ready[e] = joined[:, e * LANES : (e + 1) * LANES]
+    piece = rows // PIECES
+    slices = [[] for _ in range(PIECES)]
+    for p in range(PIECES):
+        for d in (2, 3, 1):
+            to = t + d - 2 * (t & d)
+            k = p * (times - 1) + d - 1
+            at = pl.multiple_of(to * rows + p * piece, piece)
+            copy = pltpu.make_async_remote_copy(
+                src_ref=packed.at[pl.ds(at, piece)],
+                dst_ref=landed.at[p, t],
+                send_sem=slice_send.at[k],
+                recv_sem=slice_recv.at[k],
+                device_id=(f, to),
+                device_id_type=MESH,
+            )
+            copy.start()
+            slices[p].append(copy)
+    for p in range(PIECES):
+        at = pl.multiple_of(t * rows + p * piece, piece)
+        landed[p, t] = packed[pl.ds(at, piece), :]
 
     here = spectra.at[pl.ds(pl.multiple_of(f * PATHS, PATHS), PATHS)]
     part = half // PARTS
     arrived = spread_recv.at[lax.rem(f // part, PARTS)]
 
-    def spread(j, carry):
-        k = lax.rem(j + f, 2 * group)
-        number, time = k // 2, 2 * lax.rem(k, 2) + core
-        at = pl.ds(pl.multiple_of(number // 2 * PATHS, PATHS), PATHS)
-        tile = ready.at[lax.rem(number, 2), at]
-        to = t * group + number
-        local = (to == f) & (time == t)
-
-        @pl.when(local)
-        def _():
-            pltpu.make_async_copy(tile, here, arrived).start()
-
-        @pl.when(jnp.logical_not(local))
-        def _():
-            pltpu.make_async_remote_copy(
-                src_ref=tile,
-                dst_ref=here,
-                send_sem=spread_send,
-                recv_sem=arrived,
-                device_id=(to, time),
-                device_id_type=MESH,
-            ).start()
-
-        return carry
-
-    lax.fori_loop(0, 2 * group, spread, 0)
+    for p in range(PIECES):
+        for copy in slices[p]:
+            copy.wait_recv()
+        joined = jnp.dot(
+            jnp.concatenate([landed[p, j] for j in range(times)], axis=1),
+            place[...],
+            preferred_element_type=jnp.float32,
+        ).astype(jnp.bfloat16)
+        for e in range(2):
+            ready[e, p * piece : (p + 1) * piece, :] = joined[
+                :, e * LANES : (e + 1) * LANES
+            ]
+        for n in range(p * columns // PIECES, (p + 1) * columns // PIECES):
+            for e in range(2):
+                to = t * group + far_first[n] * 2 + e
+                tile = ready.at[e, pl.ds(n * PATHS, PATHS)]
+                for across in range(2):
+                    time = 2 * across + core
+                    copy = pltpu.make_async_remote_copy(
+                        src_ref=tile,
+                        dst_ref=here,
+                        send_sem=spread_send,
+                        recv_sem=arrived,
+                        device_id=(to, time),
+                        device_id_type=MESH,
+                    )
+                    if n < columns - 1:
+                        copy.start()
+                        continue
+                    local = (to == f) & (time == t)
+                    pl.when(jnp.logical_not(local))(copy.start)
+                    pl.when(local)(pltpu.make_async_copy(tile, here, arrived).start)
 
     mate = t + 1 - 2 * mine
     shared = []
@@ -313,7 +327,7 @@
         )
         copy.start()
         shared.append(copy)
-    for copy in slices:
+    for copy in sum(slices, []):
         copy.wait_send()
 
     def drain(count):
@@ -391,12 +405,12 @@
             pltpu.VMEM((PATHS * 2 * SLOT, LANES), jnp.float32),
             pltpu.VMEM((QUADS * PATHS, LANES), jnp.float32),
             pltpu.VMEM((QUADS * PATHS, LANES), jnp.bfloat16),
-            pltpu.VMEM((times, rows, LANES), jnp.bfloat16),
+            pltpu.VMEM((PIECES, times, rows // PIECES, LANES), jnp.bfloat16),
             pltpu.VMEM((2, rows, LANES), jnp.bfloat16),
             dma((PATHS,)),
             dma((len(tables),)),
-            dma((times - 1,)),
-            dma((times - 1,)),
+            dma((PIECES * (times - 1),)),
+            dma((PIECES * (times - 1),)),
             dma,
             dma((PARTS,)),
             dma((PARTS,)),

time: 28.5 us -> 27 us (0.947)
  Pallas kernels: 28.4 us -> 26.9 us
    pallas_call x1, Pallas kernels: 26.1 us -> 24.6 us  [run_front(): pl.pallas_call(functools.partial(front, freqs, times), out_shape=pltpu.VM...]
where the time goes in v3:
time: 27 us; the launch traced here: 26.9 us
  Pallas kernels  26.9 us (100%)
    pallas_call x1, Pallas kernels, run_front(): pl.pallas_call(functools.partial(front, freqs, times), out_shape=pltpu.VM...  24.6 us
    pallas_call x1, Pallas kernels, run_correlate(): pl.pallas_call(functools.partial(correlate, slots), out_shape=jax.ShapeDt...  2.26 us

profile of v3, /device:TPU:1, one launch (start us, length us, event | category | flops | bytes accessed | tf_op | source)
XLA Modules:
  0.0 26.9 jit_solution(3286564155576814851)
XLA Ops:
  0.0 0.0 copy-start
  0.0 24.6 %front.1.spectra = bf16[1024,128]{1,0:T(8,128)(2,1)S(1)} custom-call(s32[8192,128]{1,0:T(8,128)} %bitcast.5, f32[4,64,128]{2,1,0:T(8,128)} %constant.10.clone.window_hbm, bf16[1024,256]{1,0:T(8,128)(2,1)} %constant.11.clone.turn_hbm, f32[2,16,128]{2,1,0:T(8,128)} %constant.12.clone.runs_hbm, bf16[32,128]{1,0:T(8,128)(2,1)} %constant.13.clone.quads_hbm, ...), custom_call_target="tpu_custom_call" | custom-call | tf_op jit(solution)/shard_map/front/pallas_call | solution.py:396
  24.6 0.0 copy-done
  24.6 2.3 %correlate.1 = f32[9,2,2,128,128]{4,3,2,1,0:T(8,128)} custom-call(s32[36]{0:T(128)S(1)} %copy-done, bf16[1024,128]{1,0:T(8,128)(2,1)S(1)} %front.1.spectra), custom_call_target="tpu_custom_call" | custom-call | tf_op jit(solution)/shard_map/correlate/pallas_call | solution.py:427
Async XLA Ops:
  0.0 24.6 %copy-start = (s32[36]{0:T(128)S(1)}, s32[36]{0:T(128)}, u32[]{:S(2)}) copy-start(s32[36]{0:T(128)} %ids.1) | copy-start | bytes 436

commit v4 on v3

--- a/solution.py
+++ b/solution.py
@@ -54,10 +54,7 @@
                 [real * cosine - imag * sine, real * sine + imag * cosine], axis=1
             )
         )
-    table = np.concatenate(quarters, axis=0).astype(np.float32)
-    high = table.astype(jnp.bfloat16)
-    low = (table - high.astype(np.float32)).astype(jnp.bfloat16)
-    return np.concatenate([high, low], axis=0)
+    return np.concatenate(quarters, axis=0).astype(np.float32).astype(jnp.bfloat16)
 
 
 def run_table():
@@ -144,9 +141,10 @@
     ]
     tables[0].start()
     lax.fori_loop(0, BATCH, start_fetch, 0)
-    for table in tables[1:]:
+    for table in tables[1:4]:
         table.start()
     lax.fori_loop(BATCH, PATHS, start_fetch, 0)
+    tables[4].start()
 
     barrier = pltpu.get_barrier_semaphore()
     for d in range(1, times):
@@ -201,15 +199,10 @@
 
         @pl.when(n == 0)
         def _():
-            tables[1].wait()
-            tables[2].wait()
-
-        value = z[...]
-        u = jnp.dot(
-            jnp.concatenate([value, value], axis=1),
-            turn[...],
-            preferred_element_type=jnp.float32,
-        )
+            for table in tables[1:3]:
+                table.wait()
+
+        u = jnp.dot(z[...], turn[...], preferred_element_type=jnp.float32)
         real, imag = runs[0], runs[1]
         for path in range(BATCH):
             at = pl.multiple_of((n * BATCH + path) * 2 * SLOT, 2 * SLOT)
@@ -239,6 +232,7 @@
             preferred_element_type=jnp.float32,
         )
         mixed[pl.ds(i, QUADS, stride=PATHS), :] = moved
+
     columns = group // 2
     z_here = lax.rem(f // 2, columns)
     far_first = [

time: 27 us -> 26.4 us (0.978)
  Pallas kernels: 26.9 us -> 26.3 us
    pallas_call x1, Pallas kernels: 24.6 us -> 24 us  [run_front(): pl.pallas_call(functools.partial(front, freqs, times), out_shape=pltpu.VM...]
where the time goes in v4:
time: 26.4 us; the launch traced here: 26.3 us
  Pallas kernels  26.3 us (100%)
    pallas_call x1, Pallas kernels, run_front(): pl.pallas_call(functools.partial(front, freqs, times), out_shape=pltpu.VM...  24 us
    pallas_call x1, Pallas kernels, run_correlate(): pl.pallas_call(functools.partial(correlate, slots), out_shape=jax.ShapeDt...  2.26 us

profile of v4, /device:TPU:1, one launch (start us, length us, event | category | flops | bytes accessed | tf_op | source)
XLA Modules:
  0.0 26.3 jit_solution(10168607452683223453)
XLA Ops:
  0.0 0.0 copy-start
  0.0 24.0 %front.1.spectra = bf16[1024,128]{1,0:T(8,128)(2,1)S(1)} custom-call(s32[8192,128]{1,0:T(8,128)} %bitcast.5, f32[4,64,128]{2,1,0:T(8,128)} %constant.10.clone.window_hbm, bf16[512,256]{1,0:T(8,128)(2,1)} %constant.11.clone.turn_hbm, f32[2,16,128]{2,1,0:T(8,128)} %constant.12.clone.runs_hbm, bf16[32,128]{1,0:T(8,128)(2,1)} %constant.13.clone.quads_hbm, ...), custom_call_target="tpu_custom_call" | custom-call | tf_op jit(solution)/shard_map/front/pallas_call | solution.py:390
  24.0 0.0 copy-done
  24.0 2.3 %correlate.1 = f32[9,2,2,128,128]{4,3,2,1,0:T(8,128)} custom-call(s32[36]{0:T(128)S(1)} %copy-done, bf16[1024,128]{1,0:T(8,128)(2,1)S(1)} %front.1.spectra), custom_call_target="tpu_custom_call" | custom-call | tf_op jit(solution)/shard_map/correlate/pallas_call | solution.py:421
Async XLA Ops:
  0.0 24.0 %copy-start = (s32[36]{0:T(128)S(1)}, s32[36]{0:T(128)}, u32[]{:S(2)}) copy-start(s32[36]{0:T(128)} %ids.1) | copy-start | bytes 436

commit v5 on v4

--- a/solution.py
+++ b/solution.py
@@ -1,4 +1,5 @@
 import functools
+import itertools
 import math
 
 import jax
@@ -27,7 +28,7 @@
 SPECTRA = 32
 QUADS = CHANNELS // 4
 BATCH = 8
-PIECES = 2
+PIECES = 3
 PARTS = 4
 MESH = pl.DeviceIdType.MESH
 
@@ -116,10 +117,14 @@
 ):
     f, t = lax.axis_index("freq"), lax.axis_index("tm")
     group = freqs // times
-    rows = group // 2 * PATHS
+    rows = group * PATHS
     half = freqs // 2
     core, mine = f // half, lax.rem(t, 2)
-    among = ((f // group == t) & (core == mine)).astype(jnp.int32)
+    side, place_x = lax.rem(f, 2), t // 2
+    among = (core == mine).astype(jnp.int32)
+
+    def across(other):
+        return jnp.where(other == side, place_x, 1 - place_x)
     per_path = BLOCKS * ROWS
 
     def fetch(i):
@@ -154,11 +159,12 @@
 
     def greet(j, carry):
         source = half * mine + j
-
-        @pl.when((source != f) | (f // group != t))
+        time = 2 * across(lax.rem(source, 2)) + core
+
+        @pl.when((source != f) | (time != t))
         def _():
             pl.semaphore_signal(
-                barrier, inc=1, device_id=(source, f // group), device_id_type=MESH
+                barrier, inc=1, device_id=(source, time), device_id_type=MESH
             )
 
         return carry
@@ -243,20 +249,22 @@
         for n, column in enumerate(far_first):
             at = pl.multiple_of((to * columns + column) * PATHS, PATHS)
             tile = mixed[pl.ds(at, PATHS), :]
-            at = to * rows + n * PATHS
+            at = ((to // 2 * columns + n) * 2 + to % 2) * PATHS
             packed[at : at + PATHS, :] = tile.astype(jnp.bfloat16)
 
-    pl.semaphore_wait(barrier, times - 1 + 2 * group - among)
-    piece = rows // PIECES
-    slices = [[] for _ in range(PIECES)]
-    for p in range(PIECES):
+    pl.semaphore_wait(barrier, times - 1 + half - among)
+    cuts = sorted({0, 1, columns // 2, columns})
+    pieces = list(zip(cuts, cuts[1:]))
+    slices = [[] for _ in pieces]
+    for p, (low, high) in enumerate(pieces):
+        size = (high - low) * 2 * PATHS
         for d in (2, 3, 1):
             to = t + d - 2 * (t & d)
             k = p * (times - 1) + d - 1
-            at = pl.multiple_of(to * rows + p * piece, piece)
+            at = lax.rem(to, 2) * rows + low * 2 * PATHS
             copy = pltpu.make_async_remote_copy(
-                src_ref=packed.at[pl.ds(at, piece)],
-                dst_ref=landed.at[p, t],
+                src_ref=packed.at[pl.ds(pl.multiple_of(at, PATHS), size)],
+                dst_ref=landed.at[t, pl.ds(low * 2 * PATHS, size)],
                 send_sem=slice_send.at[k],
                 recv_sem=slice_recv.at[k],
                 device_id=(f, to),
@@ -264,46 +272,41 @@
             )
             copy.start()
             slices[p].append(copy)
-    for p in range(PIECES):
-        at = pl.multiple_of(t * rows + p * piece, piece)
-        landed[p, t] = packed[pl.ds(at, piece), :]
+    landed[t] = packed[pl.ds(pl.multiple_of(mine * rows, rows), rows), :]
 
     here = spectra.at[pl.ds(pl.multiple_of(f * PATHS, PATHS), PATHS)]
     part = half // PARTS
     arrived = spread_recv.at[lax.rem(f // part, PARTS)]
 
-    for p in range(PIECES):
+    for p, (low, high) in enumerate(pieces):
         for copy in slices[p]:
             copy.wait_recv()
+        piece = slice(low * 2 * PATHS, high * 2 * PATHS)
         joined = jnp.dot(
-            jnp.concatenate([landed[p, j] for j in range(times)], axis=1),
+            jnp.concatenate([landed[j, piece, :] for j in range(times)], axis=1),
             place[...],
             preferred_element_type=jnp.float32,
         ).astype(jnp.bfloat16)
         for e in range(2):
-            ready[e, p * piece : (p + 1) * piece, :] = joined[
-                :, e * LANES : (e + 1) * LANES
-            ]
-        for n in range(p * columns // PIECES, (p + 1) * columns // PIECES):
-            for e in range(2):
-                to = t * group + far_first[n] * 2 + e
-                tile = ready.at[e, pl.ds(n * PATHS, PATHS)]
-                for across in range(2):
-                    time = 2 * across + core
-                    copy = pltpu.make_async_remote_copy(
-                        src_ref=tile,
-                        dst_ref=here,
-                        send_sem=spread_send,
-                        recv_sem=arrived,
-                        device_id=(to, time),
-                        device_id_type=MESH,
-                    )
-                    if n < columns - 1:
-                        copy.start()
-                        continue
-                    local = (to == f) & (time == t)
-                    pl.when(jnp.logical_not(local))(copy.start)
-                    pl.when(local)(pltpu.make_async_copy(tile, here, arrived).start)
+            ready[e, piece, :] = joined[:, e * LANES : (e + 1) * LANES]
+        for n, y, e in itertools.product(range(low, high), range(2), range(2)):
+            to = (2 * mine + y) * group + far_first[n] * 2 + e
+            time = 2 * across(e) + core
+            tile = ready.at[e, pl.ds((n * 2 + y) * PATHS, PATHS)]
+            copy = pltpu.make_async_remote_copy(
+                src_ref=tile,
+                dst_ref=here,
+                send_sem=spread_send,
+                recv_sem=arrived,
+                device_id=(to, time),
+                device_id_type=MESH,
+            )
+            if n < columns - 1:
+                copy.start()
+                continue
+            local = (to == f) & (time == t)
+            pl.when(jnp.logical_not(local))(copy.start)
+            pl.when(local)(pltpu.make_async_copy(tile, here, arrived).start)
 
     mate = t + 1 - 2 * mine
     shared = []
@@ -330,11 +333,11 @@
 
     @pl.when(among == 1)
     def _():
-        drain(2 * group - 1)
+        drain(half - 1)
 
     @pl.when(among == 0)
     def _():
-        drain(2 * group)
+        drain(half)
 
     for copy in shared:
         copy.wait()
@@ -377,7 +380,7 @@
 
 
 def run_front(freqs, times, samples):
-    rows = freqs // times // 2 * PATHS
+    rows = freqs // times * PATHS
     dma = pltpu.SemaphoreType.DMA
     hbm = pl.BlockSpec(memory_space=pl.ANY)
     tables = [
@@ -399,7 +402,7 @@
             pltpu.VMEM((PATHS * 2 * SLOT, LANES), jnp.float32),
             pltpu.VMEM((QUADS * PATHS, LANES), jnp.float32),
             pltpu.VMEM((QUADS * PATHS, LANES), jnp.bfloat16),
-            pltpu.VMEM((PIECES, times, rows // PIECES, LANES), jnp.bfloat16),
+            pltpu.VMEM((times, rows, LANES), jnp.bfloat16),
             pltpu.VMEM((2, rows, LANES), jnp.bfloat16),
             dma((PATHS,)),
             dma((len(tables),)),

time: 26.4 us -> 26.3 us (level)
  no operation moved by 1% of the time
where the time goes in v5:
time: 26.3 us
  Pallas kernels  26.2 us (100%)
    pallas_call x1, Pallas kernels, run_front(): pl.pallas_call(functools.partial(front, freqs, times), out_shape=pltpu.VM...  24 us
    pallas_call x1, Pallas kernels, run_correlate(): pl.pallas_call(functools.partial(correlate, slots), out_shape=jax.ShapeDt...  2.26 us

profile of v5, /device:TPU:1, one launch (start us, length us, event | category | flops | bytes accessed | tf_op | source)
XLA Modules:
  0.0 26.3 jit_solution(16061702443448768088)
XLA Ops:
  0.0 0.0 copy-start
  0.0 24.0 %front.1.spectra = bf16[1024,128]{1,0:T(8,128)(2,1)S(1)} custom-call(s32[8192,128]{1,0:T(8,128)} %bitcast.5, f32[4,64,128]{2,1,0:T(8,128)} %constant.10.clone.window_hbm, bf16[512,256]{1,0:T(8,128)(2,1)} %constant.11.clone.turn_hbm, f32[2,16,128]{2,1,0:T(8,128)} %constant.12.clone.runs_hbm, bf16[32,128]{1,0:T(8,128)(2,1)} %constant.13.clone.quads_hbm, ...), custom_call_target="tpu_custom_call" | custom-call | tf_op jit(solution)/shard_map/front/pallas_call | solution.py:393
  24.0 0.0 copy-done
  24.0 2.3 %correlate.1 = f32[9,2,2,128,128]{4,3,2,1,0:T(8,128)} custom-call(s32[36]{0:T(128)S(1)} %copy-done, bf16[1024,128]{1,0:T(8,128)(2,1)S(1)} %front.1.spectra), custom_call_target="tpu_custom_call" | custom-call | tf_op jit(solution)/shard_map/correlate/pallas_call | solution.py:424
Async XLA Ops:
  0.0 24.0 %copy-start = (s32[36]{0:T(128)S(1)}, s32[36]{0:T(128)}, u32[]{:S(2)}) copy-start(s32[36]{0:T(128)} %ids.1) | copy-start | bytes 436

commit v6 on v5

--- a/solution.py
+++ b/solution.py
@@ -146,30 +146,37 @@
     ]
     tables[0].start()
     lax.fori_loop(0, BATCH, start_fetch, 0)
+    columns = group // 2
+    z_here = lax.rem(f // 2, columns)
+    far_first = [
+        lax.rem(z_here + d, columns)
+        for d in sorted(range(columns), key=lambda d: -min(d, columns - d))
+    ]
+
+    barrier = pltpu.get_barrier_semaphore()
+    for n, y, e in itertools.product(range(columns), range(2), range(2)):
+        source = (2 * mine + y) * group + far_first[n] * 2 + e
+        time = 2 * across(e) + core
+        greet = functools.partial(
+            pl.semaphore_signal,
+            barrier,
+            inc=1,
+            device_id=(source, time),
+            device_id_type=MESH,
+        )
+        if n < columns - 1:
+            greet()
+        else:
+            pl.when((source != f) | (time != t))(greet)
+    for d in range(1, times):
+        pl.semaphore_signal(
+            barrier, inc=1, device_id=(f, lax.rem(t + d, times)), device_id_type=MESH
+        )
     for table in tables[1:4]:
         table.start()
     lax.fori_loop(BATCH, PATHS, start_fetch, 0)
     tables[4].start()
 
-    barrier = pltpu.get_barrier_semaphore()
-    for d in range(1, times):
-        pl.semaphore_signal(
-            barrier, inc=1, device_id=(f, lax.rem(t + d, times)), device_id_type=MESH
-        )
-
-    def greet(j, carry):
-        source = half * mine + j
-        time = 2 * across(lax.rem(source, 2)) + core
-
-        @pl.when((source != f) | (time != t))
-        def _():
-            pl.semaphore_signal(
-                barrier, inc=1, device_id=(source, time), device_id_type=MESH
-            )
-
-        return carry
-
-    lax.fori_loop(0, half, greet, 0)
     sums[...] = jnp.zeros_like(sums)
 
     tables[0].wait()
@@ -239,12 +246,6 @@
         )
         mixed[pl.ds(i, QUADS, stride=PATHS), :] = moved
 
-    columns = group // 2
-    z_here = lax.rem(f // 2, columns)
-    far_first = [
-        lax.rem(z_here + d, columns)
-        for d in sorted(range(columns), key=lambda d: -min(d, columns - d))
-    ]
     for to in range(times):
         for n, column in enumerate(far_first):
             at = pl.multiple_of((to * columns + column) * PATHS, PATHS)

time: 26.3 us -> 26.3 us (level)
  no operation moved by 1% of the time
where the time goes in v6:
time: 26.3 us; the launch traced here: 26.2 us
  Pallas kernels  26.2 us (100%)
    pallas_call x1, Pallas kernels, run_front(): pl.pallas_call(functools.partial(front, freqs, times), out_shape=pltpu.VM...  23.9 us
    pallas_call x1, Pallas kernels, run_correlate(): pl.pallas_call(functools.partial(correlate, slots), out_shape=jax.ShapeDt...  2.26 us

profile of v6, /device:TPU:1, one launch (start us, length us, event | category | flops | bytes accessed | tf_op | source)
XLA Modules:
  0.0 26.2 jit_solution(17464498666418698719)
XLA Ops:
  0.0 0.0 copy-start
  0.0 23.9 %front.1.spectra = bf16[1024,128]{1,0:T(8,128)(2,1)S(1)} custom-call(s32[8192,128]{1,0:T(8,128)} %bitcast.5, f32[4,64,128]{2,1,0:T(8,128)} %constant.10.clone.window_hbm, bf16[512,256]{1,0:T(8,128)(2,1)} %constant.11.clone.turn_hbm, f32[2,16,128]{2,1,0:T(8,128)} %constant.12.clone.runs_hbm, bf16[32,128]{1,0:T(8,128)(2,1)} %constant.13.clone.quads_hbm, ...), custom_call_target="tpu_custom_call" | custom-call | tf_op jit(solution)/shard_map/front/pallas_call | solution.py:394
  23.9 0.0 copy-done
  23.9 2.3 %correlate.1 = f32[9,2,2,128,128]{4,3,2,1,0:T(8,128)} custom-call(s32[36]{0:T(128)S(1)} %copy-done, bf16[1024,128]{1,0:T(8,128)(2,1)S(1)} %front.1.spectra), custom_call_target="tpu_custom_call" | custom-call | tf_op jit(solution)/shard_map/correlate/pallas_call | solution.py:425
Async XLA Ops:
  0.0 23.9 %copy-start = (s32[36]{0:T(128)S(1)}, s32[36]{0:T(128)}, u32[]{:S(2)}) copy-start(s32[36]{0:T(128)} %ids.1) | copy-start | bytes 436

commit v7 on v6

--- a/solution.py
+++ b/solution.py
@@ -311,7 +311,9 @@
 
     mate = t + 1 - 2 * mine
     shared = []
-    for k in range(PARTS):
+    near = z_here // max(columns // 2, 1)
+    for n in range(PARTS):
+        k = n % 2 * 2 + (near if n < 2 else 1 - near)
         at = (mine * PARTS + k) * part * PATHS
         some = spectra.at[pl.ds(pl.multiple_of(at, part * PATHS), part * PATHS)]
         pltpu.make_async_copy(some, some, spread_recv.at[k]).wait()

time: 26.3 us -> 26.2 us (level)
  no operation moved by 1% of the time
where the time goes in v7:
time: 26.2 us
  Pallas kernels  26.1 us (100%)
    pallas_call x1, Pallas kernels, run_front(): pl.pallas_call(functools.partial(front, freqs, times), out_shape=pltpu.VM...  23.9 us
    pallas_call x1, Pallas kernels, run_correlate(): pl.pallas_call(functools.partial(correlate, slots), out_shape=jax.ShapeDt...  2.26 us

profile of v7, /device:TPU:1, one launch (start us, length us, event | category | flops | bytes accessed | tf_op | source)
XLA Modules:
  0.0 26.2 jit_solution(10968046122216168320)
XLA Ops:
  0.0 0.0 copy-start
  0.0 23.9 %front.1.spectra = bf16[1024,128]{1,0:T(8,128)(2,1)S(1)} custom-call(s32[8192,128]{1,0:T(8,128)} %bitcast.5, f32[4,64,128]{2,1,0:T(8,128)} %constant.10.clone.window_hbm, bf16[512,256]{1,0:T(8,128)(2,1)} %constant.11.clone.turn_hbm, f32[2,16,128]{2,1,0:T(8,128)} %constant.12.clone.runs_hbm, bf16[32,128]{1,0:T(8,128)(2,1)} %constant.13.clone.quads_hbm, ...), custom_call_target="tpu_custom_call" | custom-call | tf_op jit(solution)/shard_map/front/pallas_call | solution.py:396
  23.9 0.0 copy-done
  23.9 2.3 %correlate.1 = f32[9,2,2,128,128]{4,3,2,1,0:T(8,128)} custom-call(s32[36]{0:T(128)S(1)} %copy-done, bf16[1024,128]{1,0:T(8,128)(2,1)S(1)} %front.1.spectra), custom_call_target="tpu_custom_call" | custom-call | tf_op jit(solution)/shard_map/correlate/pallas_call | solution.py:427
Async XLA Ops:
  0.0 23.9 %copy-start = (s32[36]{0:T(128)S(1)}, s32[36]{0:T(128)}, u32[]{:S(2)}) copy-start(s32[36]{0:T(128)} %ids.1) | copy-start | bytes 436
